TPU v7x, 256 devices: a whole 4x4x8 slice. The times are simulated.
256 devices in a mesh: inner: 32 (over x_lo, z, core), outer: 8 (over x_hi, y).
Axes of the slice: x: 4 (x_hi: 2, x_lo: 2; x = x_hi * 2 + x_lo), y: 4, z: 8, core: 2. Of those that a mesh axis runs over, the one named last changes fastest.
Arguments:
- queries: float32 [8, 28672, 128], P('outer', 'inner'), may hold values from -52 to 52
- keys: float32 [8, 28672, 128], P('outer', 'inner'), may hold values from -8 to 8
- values: float32 [8, 28672, 128], P('outer', 'inner'), may hold values from -14 to 14
- out_grad: float32 [8, 28672, 128], P('outer', 'inner'), may hold values from -6 to 6
- stretch_order: int32 [8, 224], P('outer', 'inner'), may hold values from 0 to 6, as said below
Outputs:
- attn_out: float32 [8, 28672, 128], P('outer', 'inner')
- query_grad: float32 [8, 28672, 128], P('outer', 'inner')
- key_grad: float32 [8, 28672, 128], P('outer', 'inner')
- value_grad: float32 [8, 28672, 128], P('outer', 'inner')
Inputs may be any that keep to these rules, and one draw needn't show every extreme that they name: `stretch_order`: each block's 7 entries are a permutation of 0 .. 6.
All inputs are finite; a program needn't handle non-finite values.
Results may differ from a plain program's by a relative error of at most 0.0004.
Values sent between devices are 32-bit elements; how exact they have to be, the bound alone decides.
A program may use at most 128 MiB of HBM per device.

v0:
```python
import functools
import math

import jax
import jax.numpy as jnp
from jax import lax
from jax.experimental import pallas as pl
from jax.experimental.pallas import tpu as pltpu
from jax.sharding import PartitionSpec as P

F32 = jnp.float32
BF16 = jnp.bfloat16
TOK = 896
D = 128
ST = 128
NS = 7
GROUPS = ((0, 128), (128, 256), (384, 256), (640, 256))
NEG = -1e30
BIG = 1e30
NT = (((1,), (1,)), ((), ()))
NN = (((1,), (0,)), ((), ()))
LOG2E = math.log2(math.e)
MESH = pl.DeviceIdType.MESH


def dot(a, b, dims):
    return lax.dot_general(a, b, dims, preferred_element_type=F32)


def split(x):
    high = x.astype(BF16)
    low = (x - high.astype(F32)).astype(BF16)
    return high, low


def dot_nt(left, right):
    return dot(left, jnp.concatenate([right, right[:, :D]], axis=1), NT)


def dot_nn(x, right):
    high, low = split(x)
    return dot(high, right, NN) + dot(low, right, NN)


def kernel(
    total_devices,
    comm,
    q_ref, k_ref, v_ref, g_ref,
    o_out, dq_out, dk_out, dv_out,
    own, recv,
    own_a, own_b, far_a, mid,
    s0, s1, s2, s3, e0, e1, e2, e3,
    s12, p12, st12, pt12,
    m_acc, l_acc, o_acc, dk_acc, dv_acc,
    lse_c, del_c, stats, stats_in, dsh, dsl,
    send_sem, recv_sem, st_send, st_recv,
):
    s_own = (s0, s1, s2, s3)
    s_far = (e0, e1, e2, e3)
    if comm:
        n_inner = lax.axis_size("inner")
        g = lax.axis_index("outer") * n_inner + lax.axis_index("inner")

        def device(delta):
            t = lax.rem(g + delta + total_devices, total_devices)
            return {"outer": t // n_inner, "inner": lax.rem(t, n_inner)}

        barrier = pltpu.get_barrier_semaphore()
        for delta in (-3, -2, -1, 1, 2, 3):
            pl.semaphore_signal(barrier, inc=1, device_id=device(delta), device_id_type=MESH)
    else:
        g = 5
    par = lax.rem(g, 2)
    sgn = 1 - 2 * par

    own[0, 0] = k_ref[0]
    own[0, 1] = v_ref[0]
    own[1, 0] = q_ref[0] * (LOG2E / math.sqrt(D))
    own[1, 1] = g_ref[0]

    def copy(src, dst, u, delta, send, rsem):
        r0, n = GROUPS[u] if isinstance(u, int) else (pl.multiple_of(256 * u - 128, 128), 256)
        return pltpu.make_async_remote_copy(
            src_ref=src.at[:, pl.ds(r0, n), :],
            dst_ref=dst.at[:, pl.ds(r0, n), :],
            send_sem=send, recv_sem=rsem,
            device_id=device(delta), device_id_type=MESH,
        )

    def make(kind, u):
        if kind == 0:
            return copy(own.at[1 - par], recv.at[1 - par, 0], u, -sgn, send_sem.at[0, u], recv_sem.at[1 - par, 0, u])
        if kind == 1:
            return copy(own.at[par], recv.at[par, 1], u, 2 * sgn, send_sem.at[1, u], recv_sem.at[par, 1, u])
        if kind == 2:
            return copy(own.at[par], recv.at[par, 0], u, sgn, send_sem.at[2, u], recv_sem.at[par, 0, u])
        if kind == 3:
            return copy(recv.at[par, 0], recv.at[par, 1], u, sgn, send_sem.at[3, u], recv_sem.at[par, 1, u])
        if kind == 4:
            return copy(recv.at[par, 0], recv.at[par, 2], u, 2 * sgn, send_sem.at[4, u], recv_sem.at[par, 2, u])
        return copy(recv.at[par, 1], recv.at[par, 2], u, sgn, send_sem.at[5, u], recv_sem.at[par, 2, u])

    def arrived(a, d, u):
        copy(own.at[a], recv.at[a, d], u, 1, send_sem.at[0, u], recv_sem.at[a, d, u]).wait_recv()

    if comm:
        pl.semaphore_wait(barrier, 6)
        for u in range(4):
            make(0, u).start()
            make(1, u).start()
            make(2, u).start()

    def near(u):
        if not comm:
            return
        arrived(par, 0, u)
        make(3, u).start()
        make(4, u).start()
        arrived(par, 1, u)
        make(5, u).start()
        arrived(1 - par, 0, u)
        arrived(1 - par, 1, u)

    for a in range(2):
        for w in range(2):
            high, low = split(own[a, w])
            own_a[a, w, :, 0:D] = high
            own_a[a, w, :, D:2 * D] = low
            own_b[a, w, :, 0:D] = high
            own_b[a, w, :, D:2 * D] = high
            own_b[a, w, :, 2 * D:3 * D] = low

    m_acc[...] = jnp.full_like(m_acc, NEG)
    l_acc[...] = jnp.zeros_like(l_acc)
    o_acc[...] = jnp.zeros_like(o_acc)
    dk_acc[...] = jnp.zeros_like(dk_acc)
    dv_acc[...] = jnp.zeros_like(dv_acc)

    def diag(n, strict):
        row = lax.broadcasted_iota(jnp.int32, (n, n), 0)
        col = lax.broadcasted_iota(jnp.int32, (n, n), 1)
        return (row, col)

    def q_tile(r0, n, ka, va, store, valid, mask):
        rows = slice(r0, r0 + n)
        width = ka.shape[0]
        s = mask(dot_nt(own_b[1, 0, rows, :], ka))
        store[...] = s
        top = s[:, :D] if width == D else jnp.maximum(s[:, :D], s[:, D:])
        top = jnp.max(top, axis=1, keepdims=True)
        old = m_acc[rows, :]
        if valid is not None:
            top = jnp.where(valid, top, NEG)
        new = jnp.maximum(old, top)
        use = new if valid is None else jnp.where(valid, new, BIG)
        alpha = jnp.exp2(old - new)
        m_acc[rows, :] = new
        halves = []
        total = l_acc[rows, :] * alpha
        for h in range(width // D):
            e = jnp.exp2(s[:, h * D:(h + 1) * D] - use)
            total = total + e
            halves.append(e)
        l_acc[rows, :] = total
        e = halves[0] if width == D else jnp.concatenate(halves, axis=1)
        add = dot_nn(e, va)
        o_acc[rows, 0:D] = o_acc[rows, 0:D] * alpha + add[:, 0:D]
        o_acc[rows, D:2 * D] = o_acc[rows, D:2 * D] * alpha + add[:, D:2 * D]

    def same(s):
        return s

    def own_mask(n):
        def mask(s):
            if s.shape[0] == n:
                top, rest = s, None
            else:
                top, rest = s[:n], s[n:]
            row = lax.broadcasted_iota(jnp.int32, (n, n), 0)
            col = lax.broadcasted_iota(jnp.int32, (n, n), 1)
            top = jnp.where(col <= row, top, NEG)
            return top if rest is None else jnp.concatenate([top, rest], axis=0)
        return mask

    def far_mask(n):
        def mask(s):
            m = s.shape[0] - n
            row = lax.broadcasted_iota(jnp.int32, (n, n), 0)
            col = lax.broadcasted_iota(jnp.int32, (n, n), 1)
            last = jnp.where(col > row, s[m:], NEG)
            return last if m == 0 else jnp.concatenate([s[:m], last], axis=0)
        return mask

    for u, (r0, n) in enumerate(GROUPS):
        q_tile(r0, TOK - r0, own_a[0, 0, r0:r0 + n, :], own_a[0, 1, r0:r0 + n, :], s_own[u], None, own_mask(n))

    def put(t, half, a, d, r0, n):
        for w in range(2):
            high, low = split(recv[a, d, w, pl.ds(r0, n), :])
            mid[a, w, t, half:half + n, 0:D] = high
            mid[a, w, t, half:half + n, D:2 * D] = low

    def tile(t, valid, mask):
        q_tile(0, TOK, mid[0, 0, t], mid[0, 1, t], s12.at[t], valid, mask)
        p12[t] = dot_nt(own_b[1, 1], mid[0, 1, t])
        st12[t] = dot_nt(own_b[0, 0], mid[1, 0, t])
        pt12[t] = dot_nt(own_b[0, 1], mid[1, 1, t])

    near(0)
    for a in range(2):
        put(0, 0, a, 0, 0, ST)
        put(0, ST, a, 1, 0, ST)

    def both(s):
        return jnp.concatenate([jnp.where(g >= 1, s[:, :D], NEG), jnp.where(g >= 2, s[:, D:], NEG)], axis=1)

    tile(0, None, both)

    def step(u, carry):
        near(u)
        r0 = pl.multiple_of(256 * u - 128, 128)
        for d in range(2):
            t = 2 * u - 1 + d
            for a in range(2):
                put(t, 0, a, d, r0, 256)
            tile(t, g >= d + 1, same)
        return carry

    lax.fori_loop(1, 4, step, 0)

    def keys_side(q_rows, lse, dlt, scores, dprobs, ga, qa, rows):
        pt = jnp.exp2(scores - lse)
        dv_acc[rows, :] += dot_nn(pt, ga)
        dk_acc[rows, :] += dot_nn(pt * (dprobs - dlt), qa)

    for u in (3, 2, 1, 0):
        r0, n = GROUPS[u]
        rows = slice(r0, r0 + n)
        if comm:
            arrived(0, 2, u)
        for w in range(2):
            high, low = split(recv[0, 2, w, rows, :])
            far_a[0, w, rows, 0:D] = high
            far_a[0, w, rows, D:2 * D] = low
        q_tile(0, r0 + n, far_a[0, 0, rows, :], far_a[0, 1, rows, :], s_far[u], g >= 3, far_mask(n))
        total = jnp.sum(l_acc[rows, :], axis=1, keepdims=True)
        out = (o_acc[rows, 0:D] + o_acc[rows, D:2 * D]) / total
        o_acc[rows, 0:D] = out
        delta = jnp.sum(own[1, 1, rows, :] * out, axis=1, keepdims=True)
        lse = m_acc[rows, :] + jnp.log2(total)
        delta = jnp.broadcast_to(delta, (n, D))
        for j in range(n // ST):
            part = slice(j * ST, (j + 1) * ST)
            cols = slice(r0 + j * ST, r0 + (j + 1) * ST)
            stats[0, :, cols] = jnp.transpose(lse[part])[0:8]
            stats[1, :, cols] = jnp.transpose(delta[part])[0:8]

        def stat_copy(d):
            return pltpu.make_async_remote_copy(
                src_ref=stats.at[:, :, pl.ds(r0, n)],
                dst_ref=stats_in.at[d, :, :, pl.ds(r0, n)],
                send_sem=st_send.at[d, u], recv_sem=st_recv.at[d, u],
                device_id=device(-(d + 1)), device_id_type=MESH,
            )

        if comm:
            for d in range(3):
                stat_copy(d).start()
            arrived(1, 2, u)
        for w in range(2):
            high, low = split(recv[1, 2, w, rows, :])
            far_a[1, w, rows, 0:D] = high
            far_a[1, w, rows, D:2 * D] = low

        def ds_part(s, dp, use):
            return split(jnp.exp2(s - use) * (dp - delta[:, :1]))

        lse1 = lse[:, :1]
        for t in range(7):
            if t == 0:
                use = lse1
            else:
                use = jnp.where(g >= 1 + (t - 1) % 2, lse1, BIG)
            high, low = ds_part(s12[t, rows, :], p12[t, rows, :], use)
            dsh[0:n, t * 256:(t + 1) * 256] = high
            dsl[0:n, t * 256:(t + 1) * 256] = low
        k12 = mid[0, 0].reshape(7 * 256, 256)
        dq = dot(dsh[0:n, :], k12, NN) + dot(dsl[0:n, :], k12, NN)
        for v, (c0, w) in enumerate(GROUPS):
            cols = slice(c0, c0 + w)
            if v <= u:
                s = s_own[v][r0 - c0:r0 - c0 + n, :]
                dp = dot_nt(own_b[1, 1, rows, :], own_a[0, 1, cols, :])
                high, low = ds_part(s, dp, lse1)
                ka = own_a[0, 0, cols, :]
                dq = dq + dot(high, ka, NN) + dot(low, ka, NN)
            if v >= u:
                s = s_far[v][rows, :]
                dp = dot_nt(own_b[1, 1, rows, :], far_a[0, 1, cols, :])
                high, low = ds_part(s, dp, jnp.where(g >= 3, lse1, BIG))
                ka = far_a[0, 0, cols, :]
                dq = dq + dot(high, ka, NN) + dot(low, ka, NN)
        dq_out[0, rows, :] = (dq[:, :D] + dq[:, D:]) * (1.0 / math.sqrt(D))

        m = r0 + n
        ka = own_a[1, 0, rows, :]
        ga = own_a[1, 1, rows, :]
        scores = dot_nt(own_b[0, 0, 0:m, :], ka)
        row = lax.broadcasted_iota(jnp.int32, (n, n), 0)
        col = lax.broadcasted_iota(jnp.int32, (n, n), 1)
        last = jnp.where(row <= col, scores[m - n:], NEG)
        scores = last if m == n else jnp.concatenate([scores[:m - n], last], axis=0)
        dprobs = dot_nt(own_b[0, 1, 0:m, :], ga)
        keys_side(rows, stats[0, 0:1, rows], stats[1, 0:1, rows], scores, dprobs, ga, ka, slice(0, m))
        ka = far_a[1, 0, rows, :]
        ga = far_a[1, 1, rows, :]
        scores = dot_nt(own_b[0, 0, r0:TOK, :], ka)
        first = jnp.where(row > col, scores[:n], NEG)
        scores = first if r0 + n == TOK else jnp.concatenate([first, scores[n:]], axis=0)
        dprobs = dot_nt(own_b[0, 1, r0:TOK, :], ga)
        if comm:
            for d in range(3):
                stat_copy(d).wait_recv()
        last_dev = total_devices - 1
        use = jnp.where(g + 3 <= last_dev, stats_in[2, 0, 0:1, rows], BIG)
        keys_side(rows, use, stats_in[2, 1, 0:1, rows], scores, dprobs, ga, ka, slice(r0, TOK))
        lses = [jnp.where(g + 1 + d <= last_dev, stats_in[d, 0, 0:1, rows], BIG) for d in range(2)]
        dels = [stats_in[d, 1, 0:1, rows] for d in range(2)]
        if u == 0:
            keys_side(
                rows, jnp.concatenate(lses, axis=1), jnp.concatenate(dels, axis=1),
                st12[0], pt12[0], mid[1, 1, 0], mid[1, 0, 0], slice(0, TOK),
            )
        else:
            for d in range(2):
                t = 2 * u - 1 + d
                keys_side(rows, lses[d], dels[d], st12[t], pt12[t], mid[1, 1, t], mid[1, 0, t], slice(0, TOK))

    o_out[0] = o_acc[:, 0:D]
    dk_out[0] = (dk_acc[:, 0:D] + dk_acc[:, D:2 * D]) * (1.0 / LOG2E)
    dv_out[0] = dv_acc[:, 0:D] + dv_acc[:, D:2 * D]

    if comm:
        for u in range(4):
            for kind in range(6):
                make(kind, u).wait_send()
            r0, n = GROUPS[u]
            for d in range(3):
                pltpu.make_async_remote_copy(
                    src_ref=stats.at[:, :, pl.ds(r0, n)],
                    dst_ref=stats_in.at[d, :, :, pl.ds(r0, n)],
                    send_sem=st_send.at[d, u], recv_sem=st_recv.at[d, u],
                    device_id=device(-(d + 1)), device_id_type=MESH,
                ).wait_send()


def place(order_ref, c):
    return pl.multiple_of(order_ref[0, c] * ST, ST)


def sort_kernel(order_ref, *refs):
    for c in range(NS):
        for src, dst in zip(refs[:4], refs[4:]):
            dst[0, pl.ds(place(order_ref, c), ST), :] = src[0, c * ST:(c + 1) * ST, :]


def unsort_kernel(order_ref, *refs):
    for c in range(NS):
        for src, dst in zip(refs[:4], refs[4:]):
            dst[0, c * ST:(c + 1) * ST, :] = src[0, pl.ds(place(order_ref, c), ST), :]


def attention(total_devices, comm, queries, keys, values, out_grad, stretch_order):
    vmem = pl.BlockSpec(memory_space=pltpu.VMEM)
    smem = pl.BlockSpec(memory_space=pltpu.SMEM)
    blk = jax.ShapeDtypeStruct((1, TOK, D), F32)
    own_sizes = [(TOK - r0, n) for r0, n in GROUPS]
    far_sizes = [(r0 + n, n) for r0, n in GROUPS]
    V = pltpu.VMEM
    scratch = [
        V((2, 2, TOK, D), F32), V((2, 3, 2, TOK, D), F32),
        V((2, 2, TOK, 2 * D), BF16), V((2, 2, TOK, 3 * D), BF16), V((2, 2, TOK, 2 * D), BF16),
        V((2, 2, 7, 256, 2 * D), BF16),
    ]
    scratch += [V(s, F32) for s in own_sizes] + [V(s, F32) for s in far_sizes]
    scratch += [V((7, TOK, 256), F32)] * 4
    scratch += [V((TOK, D), F32)] * 2 + [V((TOK, 2 * D), F32)] * 3
    scratch += [V((8, 128), F32)] * 2
    scratch += [V((2, 8, TOK), F32), V((3, 2, 8, TOK), F32)]
    scratch += [V((256, 7 * 256), BF16)] * 2
    scratch += [
        pltpu.SemaphoreType.DMA((6, 4)), pltpu.SemaphoreType.DMA((2, 3, 4)),
        pltpu.SemaphoreType.DMA((3, 4)), pltpu.SemaphoreType.DMA((3, 4)),
    ]
    params = dict(vmem_limit_bytes=63 * 2**20)
    if comm:
        params.update(collective_id=0, has_side_effects=True)
    def reorder(body, name, arrays):
        return pl.pallas_call(
            body, out_shape=[blk] * 4, in_specs=[smem] + [vmem] * 4, out_specs=[vmem] * 4, name=name,
        )(stretch_order, *arrays)

    ordered = reorder(sort_kernel, "by_position", (queries, keys, values, out_grad))
    results = pl.pallas_call(
        functools.partial(kernel, total_devices, comm),
        out_shape=[blk] * 4,
        in_specs=[vmem] * 4,
        out_specs=[vmem] * 4,
        scratch_shapes=scratch,
        compiler_params=pltpu.CompilerParams(**params),
        name="windowed_attention",
    )(*ordered)
    return reorder(unsort_kernel, "by_array", results)


def solution(mesh):
    spec = P("outer", "inner", None)
    total = mesh.shape["outer"] * mesh.shape["inner"]
    return jax.shard_map(
        functools.partial(attention, total, True), mesh=mesh,
        in_specs=(spec, spec, spec, spec, P("outer", "inner")),
        out_specs=(spec,) * 4, check_vma=False,
    )
```

profile of v0, /device:TPU:1, one launch (start us, length us, event | category | flops | bytes accessed | tf_op | source)
XLA Modules:
  0.0 72.8 jit_solution(5734666917385260493)
XLA Ops:
  0.6 2.8 %by_position.1 = (f32[1,896,128]{2,1,0:T(8,128)}, f32[1,896,128]{2,1,0:T(8,128)}, f32[1,896,128]{2,1,0:T(8,128)}, f32[1,896,128]{2,1,0:T(8,128)}) custom-call(s32[1,7]{1,0:T(1,128)} %order_ref.3, f32[1,896,128]{2,1,0:T(8,128)} %refs_0_.1, f32[1,896,128]{2,1,0:T(8,128)} %refs_1_.1, f32[1,896,128]{2,1,0:T(8,128)} %refs_2_.1, f32[1,896,128]{2,1,0:T(8,128)} %refs_3_.1), custom_call_target="tpu_custom_call" | custom-call | tf_op jit(solution)/shard_map/by_position/pallas_call | solution.py:399
  3.4 66.6 %windowed_attention.1 = (f32[1,896,128]{2,1,0:T(8,128)}, f32[1,896,128]{2,1,0:T(8,128)}, f32[1,896,128]{2,1,0:T(8,128)}, f32[1,896,128]{2,1,0:T(8,128)}) custom-call(f32[1,896,128]{2,1,0:T(8,128)} %get-tuple-element.12.q_ref, f32[1,896,128]{2,1,0:T(8,128)} %get-tuple-element.13.k_ref, f32[1,896,128]{2,1,0:T(8,128)} %get-tuple-element.14.v_ref, ...), custom_call_target="tpu_custom_call" | custom-call | tf_op jit(solution)/shard_map/windowed_attention/pallas_call | solution.py:404
  70.0 2.8 %by_array.1 = (f32[1,896,128]{2,1,0:T(8,128)}, f32[1,896,128]{2,1,0:T(8,128)}, f32[1,896,128]{2,1,0:T(8,128)}, f32[1,896,128]{2,1,0:T(8,128)}) custom-call(s32[1,7]{1,0:T(1,128)} %order_ref.3, f32[1,896,128]{2,1,0:T(8,128)} %get-tuple-element.16.refs_0_, f32[1,896,128]{2,1,0:T(8,128)} %get-tuple-element.17.refs_1_, ...), custom_call_target="tpu_custom_call" | custom-call | tf_op jit(solution)/shard_map/by_array/pallas_call | solution.py:399
where the time goes:
time: 72.9 us; the launch traced here: 72.8 us
  Pallas kernels  72.1 us (99%)
    pallas_call x1, Pallas kernels, attention(): pl.pallas_call(functools.partial(kernel, total_devices, comm), out_shape=...  66.6 us
    pallas_call x2, Pallas kernels, reorder(): pl.pallas_call(body, out_shape=[blk] * 4, in_specs=[smem] + [vmem] * 4, o...  5.56 us

commit v1 on v0

v1 whole, which is shorter than its diff:
```python
import functools
import math

import jax
import jax.numpy as jnp
from jax import lax
from jax.experimental import pallas as pl
from jax.experimental.pallas import tpu as pltpu
from jax.sharding import PartitionSpec as P

F32 = jnp.float32
BF16 = jnp.bfloat16
TOK = 896
D = 128
ST = 128
NS = 7
GROUPS = ((0, 128), (128, 256), (384, 256), (640, 256))
NEG = -1e30
BIG = 1e30
NT = (((1,), (1,)), ((), ()))
NN = (((1,), (0,)), ((), ()))
LOG2E = math.log2(math.e)
MESH = pl.DeviceIdType.MESH


def dot(a, b, dims):
    return lax.dot_general(a, b, dims, preferred_element_type=F32)


def split(x):
    high = x.astype(BF16)
    low = (x - high.astype(F32)).astype(BF16)
    return high, low


def dot_nt(left, right):
    return dot(left, jnp.concatenate([right, right[:, :D]], axis=1), NT)


def dot_nn(x, right):
    high, low = split(x)
    return dot(high, right, NN) + dot(low, right, NN)


def kernel(
    total_devices,
    comm,
    order_ref, q_hbm, k_hbm, v_hbm, g_hbm,
    o_hbm, dq_hbm, dk_hbm, dv_hbm,
    stage, own, recv,
    own_a, own_b, far_a, mid,
    s0, s1, s2, s3, e0, e1, e2, e3,
    p0, p1, p2, p3, st0, st1, st2, st3, pt0, pt1, pt2, pt3,
    s12, p12, st12, pt12,
    m_acc, l_acc, o_acc, dk_acc, dv_acc,
    lse_c, del_c, stats, stats_in, dsh, dsl,
    send_sem, recv_sem, st_send, st_recv, in_sem, out_sem,
):
    s_own = (s0, s1, s2, s3)
    s_far = (e0, e1, e2, e3)
    p_own = (p0, p1, p2, p3)
    st_own = (st0, st1, st2, st3)
    pt_own = (pt0, pt1, pt2, pt3)
    if comm:
        n_inner = lax.axis_size("inner")
        g = lax.axis_index("outer") * n_inner + lax.axis_index("inner")

        def device(delta):
            t = lax.rem(g + delta + total_devices, total_devices)
            return {"outer": t // n_inner, "inner": lax.rem(t, n_inner)}

        def inside(*deltas):
            low, high = min(deltas), max(deltas)
            return jnp.logical_and(g + low >= 0, g + high < total_devices)

        barrier = pltpu.get_barrier_semaphore()

        def greet(delta):
            pl.semaphore_signal(barrier, inc=1, device_id=device(delta), device_id_type=MESH)

        for delta in (-3, -2, -1, 1, 2, 3):
            pl.when(inside(delta))(functools.partial(greet, delta))
    else:
        g = 5
    par = lax.rem(g, 2)
    sgn = 1 - 2 * par

    loads = [
        pltpu.make_async_copy(ref, stage.at[i], in_sem.at[i])
        for i, ref in enumerate((k_hbm, v_hbm, q_hbm, g_hbm))
    ]
    for load in loads:
        load.start()

    def source(s):
        total = 0
        unit = 1
        for k in range(NS):
            if k != s:
                unit = unit * (s - k)
        for c in range(1, NS):
            term = c
            for k in range(NS):
                if k != s:
                    term = term * (order_ref[0, c] - k)
            total = total + term
        return lax.rem(lax.div(total, jnp.int32(unit)), jnp.int32(NS))

    places = [source(s) for s in range(NS)]
    for load in loads:
        load.wait()
    for s in range(NS):
        rows = slice(s * ST, (s + 1) * ST)
        own[0, 0, rows, :] = stage[0, places[s]]
        own[0, 1, rows, :] = stage[1, places[s]]
        own[1, 0, rows, :] = stage[2, places[s]] * (LOG2E / math.sqrt(D))
        own[1, 1, rows, :] = stage[3, places[s]]

    def copy(src, dst, u, delta, send, rsem):
        r0, n = GROUPS[u] if isinstance(u, int) else (pl.multiple_of(256 * u - 128, 128), 256)
        return pltpu.make_async_remote_copy(
            src_ref=src.at[:, pl.ds(r0, n), :],
            dst_ref=dst.at[:, pl.ds(r0, n), :],
            send_sem=send, recv_sem=rsem,
            device_id=device(delta), device_id_type=MESH,
        )

    def make(kind, u):
        if kind == 0:
            return copy(own.at[1 - par], recv.at[1 - par, 0], u, -sgn, send_sem.at[0, u], recv_sem.at[1 - par, 0, u])
        if kind == 1:
            return copy(own.at[par], recv.at[par, 1], u, 2 * sgn, send_sem.at[1, u], recv_sem.at[par, 1, u])
        if kind == 2:
            return copy(own.at[par], recv.at[par, 0], u, sgn, send_sem.at[2, u], recv_sem.at[par, 0, u])
        if kind == 3:
            return copy(recv.at[par, 0], recv.at[par, 1], u, sgn, send_sem.at[3, u], recv_sem.at[par, 1, u])
        if kind == 4:
            return copy(recv.at[par, 0], recv.at[par, 2], u, 2 * sgn, send_sem.at[4, u], recv_sem.at[par, 2, u])
        return copy(recv.at[par, 1], recv.at[par, 2], u, sgn, send_sem.at[5, u], recv_sem.at[par, 2, u])

    def exists(kind):
        carried, to = ((0, -1), (0, 2), (0, 1), (-1, 1), (-1, 2), (-2, 1))[kind]
        first, second = g + sgn * carried, g + sgn * to
        return jnp.logical_and(
            jnp.minimum(first, second) >= 0, jnp.maximum(first, second) < total_devices
        )

    def start(*which):
        for kind, u in which:
            pl.when(exists(kind))(make(kind, u).start)

    def wait_sent(kind, u):
        pl.when(exists(kind))(make(kind, u).wait_send)

    def arrived(a, d, u):
        block = g + (2 * a - 1) * (d + 1)
        here = jnp.logical_and(block >= 0, block < total_devices)
        pl.when(here)(
            copy(own.at[a], recv.at[a, d], u, 1, send_sem.at[0, u], recv_sem.at[a, d, u]).wait_recv
        )

    if comm:
        pl.semaphore_wait(barrier, jnp.minimum(g, 3) + jnp.minimum(total_devices - 1 - g, 3))
        for u in (0, 3):
            start((0, u), (1, u))
        start((2, 0), (2, 3), (2, 2), (2, 1))

    def near(u):
        if not comm:
            return
        arrived(par, 0, u)
        start((3, u))
        if isinstance(u, int):
            start((0, 2), (1, 2))
        else:
            pl.when(u == 3)(lambda: start((0, 1), (1, 1)))
            pl.when(u == 2)(lambda: start((4, 3)))
            pl.when(u == 1)(lambda: start((4, 2)))
        arrived(par, 1, u)
        start((5, u))
        arrived(1 - par, 0, u)

    def last_near(u):
        if comm:
            arrived(1 - par, 1, u)

    for a in range(2):
        for w in range(2):
            high, low = split(own[a, w])
            own_a[a, w, :, 0:D] = high
            own_a[a, w, :, D:2 * D] = low
            own_b[a, w, :, 0:D] = high
            own_b[a, w, :, D:2 * D] = high
            own_b[a, w, :, 2 * D:3 * D] = low

    if comm:
        def clear(a, d):
            recv[a, d] = jnp.zeros((2, TOK, D), F32)

        for d in range(3):
            pl.when(g < d + 1)(functools.partial(clear, 0, d))
            pl.when(g > total_devices - 2 - d)(functools.partial(clear, 1, d))

    m_acc[...] = jnp.full_like(m_acc, NEG)
    l_acc[...] = jnp.zeros_like(l_acc)
    o_acc[...] = jnp.zeros_like(o_acc)
    dk_acc[...] = jnp.zeros_like(dk_acc)
    dv_acc[...] = jnp.zeros_like(dv_acc)

    def diag(n, strict):
        row = lax.broadcasted_iota(jnp.int32, (n, n), 0)
        col = lax.broadcasted_iota(jnp.int32, (n, n), 1)
        return (row, col)

    def q_tile(r0, n, ka, va, store, valid, mask):
        rows = slice(r0, r0 + n)
        width = ka.shape[0]
        s = mask(dot_nt(own_b[1, 0, rows, :], ka))
        store[...] = s
        top = s[:, :D] if width == D else jnp.maximum(s[:, :D], s[:, D:])
        top = jnp.max(top, axis=1, keepdims=True)
        old = m_acc[rows, :]
        if valid is not None:
            top = jnp.where(valid, top, NEG)
        new = jnp.maximum(old, top)
        use = new if valid is None else jnp.where(valid, new, BIG)
        alpha = jnp.exp2(old - new)
        m_acc[rows, :] = new
        halves = []
        total = l_acc[rows, :] * alpha
        for h in range(width // D):
            e = jnp.exp2(s[:, h * D:(h + 1) * D] - use)
            total = total + e
            halves.append(e)
        l_acc[rows, :] = total
        e = halves[0] if width == D else jnp.concatenate(halves, axis=1)
        add = dot_nn(e, va)
        o_acc[rows, 0:D] = o_acc[rows, 0:D] * alpha + add[:, 0:D]
        o_acc[rows, D:2 * D] = o_acc[rows, D:2 * D] * alpha + add[:, D:2 * D]

    def same(s):
        return s

    def own_mask(n):
        def mask(s):
            if s.shape[0] == n:
                top, rest = s, None
            else:
                top, rest = s[:n], s[n:]
            row = lax.broadcasted_iota(jnp.int32, (n, n), 0)
            col = lax.broadcasted_iota(jnp.int32, (n, n), 1)
            top = jnp.where(col <= row, top, NEG)
            return top if rest is None else jnp.concatenate([top, rest], axis=0)
        return mask

    def far_mask(n):
        def mask(s):
            m = s.shape[0] - n
            row = lax.broadcasted_iota(jnp.int32, (n, n), 0)
            col = lax.broadcasted_iota(jnp.int32, (n, n), 1)
            last = jnp.where(col > row, s[m:], NEG)
            return last if m == 0 else jnp.concatenate([s[:m], last], axis=0)
        return mask

    for u, (r0, n) in enumerate(GROUPS):
        q_tile(r0, TOK - r0, own_a[0, 0, r0:r0 + n, :], own_a[0, 1, r0:r0 + n, :], s_own[u], None, own_mask(n))

        p_own[u][...] = dot_nt(own_b[1, 1, r0:TOK, :], own_a[0, 1, r0:r0 + n, :])
    for u, (r0, n) in enumerate(GROUPS):
        m = r0 + n
        row = lax.broadcasted_iota(jnp.int32, (n, n), 0)
        col = lax.broadcasted_iota(jnp.int32, (n, n), 1)
        scores = dot_nt(own_b[0, 0, 0:m, :], own_a[1, 0, r0:m, :])
        last = jnp.where(row <= col, scores[r0:], NEG)
        st_own[u][...] = last if r0 == 0 else jnp.concatenate([scores[:r0], last], axis=0)
        pt_own[u][...] = dot_nt(own_b[0, 1, 0:m, :], own_a[1, 1, r0:m, :])

    def put(t, half, a, d, r0, n):
        for w in range(2):
            high, low = split(recv[a, d, w, pl.ds(r0, n), :])
            mid[a, w, t, half:half + n, 0:D] = high
            mid[a, w, t, half:half + n, D:2 * D] = low

    def tile(t, valid, mask):
        q_tile(0, TOK, mid[0, 0, t], mid[0, 1, t], s12.at[t], valid, mask)
        p12[t] = dot_nt(own_b[1, 1], mid[0, 1, t])
        st12[t] = dot_nt(own_b[0, 0], mid[1, 0, t])
        pt12[t] = dot_nt(own_b[0, 1], mid[1, 1, t])

    def both(s):
        return jnp.concatenate([jnp.where(g >= 1, s[:, :D], NEG), jnp.where(g >= 2, s[:, D:], NEG)], axis=1)

    near(0)
    last_near(0)
    for a in range(2):
        put(0, 0, a, 0, 0, ST)
        put(0, ST, a, 1, 0, ST)
    tile(0, None, both)

    def step(i, carry):
        u = 3 - i
        near(u)
        r0 = pl.multiple_of(256 * u - 128, 128)
        for d in range(2):
            t = 2 * u - 1 + d
            if d == 1:
                last_near(u)
            for a in range(2):
                put(t, 0, a, d, r0, 256)
            tile(t, g >= d + 1, same)
        return carry

    lax.fori_loop(0, 3, step, 0)

    def put_out(i, rows, value):
        for j in range(value.shape[0] // ST):
            stage[i, rows.start // ST + j] = value[j * ST:(j + 1) * ST]

    def query_grad(r0, m):
        end = r0 + m

        def part(s, dp, first, last, valid=None):
            use = m_acc[first:last, 0:1]
            if valid is not None:
                use = jnp.where(valid, use, BIG)
            return split(jnp.exp2(s - use) * (dp - l_acc[first:last, 0:1]))

        for t in range(7):
            valid = None if t == 0 else g >= 1 + (t - 1) % 2
            high, low = part(s12[t, r0:end, :], p12[t, r0:end, :], r0, end, valid)
            dsh[0:m, t * 256:(t + 1) * 256] = high
            dsl[0:m, t * 256:(t + 1) * 256] = low
        k12 = mid[0, 0].reshape(7 * 256, 256)
        o_acc[r0:end, :] = dot(dsh[0:m, :], k12, NN) + dot(dsl[0:m, :], k12, NN)
        for v, (c0, w) in enumerate(GROUPS):
            cols = slice(c0, c0 + w)
            first, last = max(c0, r0), min(c0 + w, end)
            if first < end:
                high, low = part(s_own[v][first - c0:end - c0, :], p_own[v][first - c0:end - c0, :], first, end)
                ka = own_a[0, 0, cols, :]
                o_acc[first:end, :] += dot(high, ka, NN) + dot(low, ka, NN)
            if last > r0:
                dp = dot_nt(own_b[1, 1, r0:last, :], far_a[0, 1, cols, :])
                high, low = part(s_far[v][r0:last, :], dp, r0, last, g >= 3)
                ka = far_a[0, 0, cols, :]
                o_acc[r0:last, :] += dot(high, ka, NN) + dot(low, ka, NN)
        grad = (o_acc[r0:end, 0:D] + o_acc[r0:end, D:2 * D]) * (1.0 / math.sqrt(D))
        put_out(1, slice(r0, end), grad)

    def keys_side(q_rows, lse, dlt, scores, dprobs, ga, qa, rows):
        pt = jnp.exp2(scores - lse)
        dv_acc[rows, :] += dot_nn(pt, ga)
        dk_acc[rows, :] += dot_nn(pt * (dprobs - dlt), qa)

    def stat_copy(d, u):
        r0, n = GROUPS[u]
        return pltpu.make_async_remote_copy(
            src_ref=stats.at[:, :, pl.ds(r0, n)],
            dst_ref=stats_in.at[d, :, :, pl.ds(r0, n)],
            send_sem=st_send.at[d, u], recv_sem=st_recv.at[d, u],
            device_id=device(-(d + 1)), device_id_type=MESH,
        )

    last_dev = total_devices - 1

    def post(u):
        r0, n = GROUPS[u]
        rows = slice(r0, r0 + n)
        if comm:
            for d in range(3):
                pl.when(inside(d + 1))(stat_copy(d, u).wait_recv)
        lses = [jnp.where(g + 1 + d <= last_dev, stats_in[d, 0, 0:1, rows], BIG) for d in range(3)]
        dels = [jnp.where(g + 1 + d <= last_dev, stats_in[d, 1, 0:1, rows], 0.0) for d in range(3)]
        if u == 0:
            keys_side(
                rows, jnp.concatenate(lses[:2], axis=1), jnp.concatenate(dels[:2], axis=1),
                st12[0], pt12[0], mid[1, 1, 0], mid[1, 0, 0], slice(0, TOK),
            )
        else:
            for d in range(2):
                t = 2 * u - 1 + d
                keys_side(rows, lses[d], dels[d], st12[t], pt12[t], mid[1, 1, t], mid[1, 0, t], slice(0, TOK))
        if comm:
            arrived(1, 2, u)
        for w in range(2):
            high, low = split(recv[1, 2, w, rows, :])
            far_a[1, w, rows, 0:D] = high
            far_a[1, w, rows, D:2 * D] = low
        scores = dot_nt(own_b[0, 0, r0:TOK, :], far_a[1, 0, rows, :])
        row = lax.broadcasted_iota(jnp.int32, (n, n), 0)
        col = lax.broadcasted_iota(jnp.int32, (n, n), 1)
        first = jnp.where(row > col, scores[:n], NEG)
        scores = first if r0 + n == TOK else jnp.concatenate([first, scores[n:]], axis=0)
        dprobs = dot_nt(own_b[0, 1, r0:TOK, :], far_a[1, 1, rows, :])
        keys_side(
            rows, lses[2], dels[2], scores, dprobs,
            far_a[1, 1, rows, :], far_a[1, 0, rows, :], slice(r0, TOK),
        )

    for u in (3, 2, 1, 0):
        r0, n = GROUPS[u]
        rows = slice(r0, r0 + n)
        if comm:
            arrived(0, 2, u)
            if u == 3:
                start((4, 1), (4, 0))
        for w in range(2):
            high, low = split(recv[0, 2, w, rows, :])
            far_a[0, w, rows, 0:D] = high
            far_a[0, w, rows, D:2 * D] = low
        q_tile(0, r0 + n, far_a[0, 0, rows, :], far_a[0, 1, rows, :], s_far[u], g >= 3, far_mask(n))
        total = jnp.sum(l_acc[rows, :], axis=1, keepdims=True)
        out = (o_acc[rows, 0:D] + o_acc[rows, D:2 * D]) / total
        put_out(0, rows, out)
        delta = jnp.sum(own[1, 1, rows, :] * out, axis=1, keepdims=True)
        lse = m_acc[rows, :] + jnp.log2(total)
        delta = jnp.broadcast_to(delta, (n, D))
        for j in range(n // ST):
            part = slice(j * ST, (j + 1) * ST)
            cols = slice(r0 + j * ST, r0 + (j + 1) * ST)
            stats[0, :, cols] = jnp.transpose(lse[part])[0:8]
            stats[1, :, cols] = jnp.transpose(delta[part])[0:8]

        if comm:
            for d in range(3):
                pl.when(inside(-(d + 1)))(stat_copy(d, u).start)
        m_acc[rows, :] = lse
        l_acc[rows, :] = delta
        if u % 2 == 0:
            query_grad(r0, 512 if u else 384)

        keys_side(
            rows, stats[0, 0:1, rows], stats[1, 0:1, rows], st_own[u][...], pt_own[u][...],
            own_a[1, 1, rows, :], own_a[1, 0, rows, :], slice(0, r0 + n),
        )

    stores = [
        pltpu.make_async_copy(stage.at[i], ref, out_sem.at[i])
        for i, ref in enumerate((o_hbm, dq_hbm, dk_hbm, dv_hbm))
    ]
    stores[0].start()
    stores[1].start()
    for u in (3, 2, 1, 0):
        post(u)
    put_out(2, slice(0, TOK), (dk_acc[:, 0:D] + dk_acc[:, D:2 * D]) * (1.0 / LOG2E))
    put_out(3, slice(0, TOK), dv_acc[:, 0:D] + dv_acc[:, D:2 * D])
    stores[2].start()
    stores[3].start()

    if comm:
        for u in range(4):
            for kind in range(6):
                wait_sent(kind, u)
            for d in range(3):
                pl.when(inside(-(d + 1)))(stat_copy(d, u).wait_send)
    for store in stores:
        store.wait()


def unsort_kernel(order_ref, *refs):
    for c in range(NS):
        for src, dst in zip(refs[:4], refs[4:]):
            dst[c] = src[order_ref[0, c]]


def attention(total_devices, comm, queries, keys, values, out_grad, stretch_order):
    vmem = pl.BlockSpec(memory_space=pltpu.VMEM)
    smem = pl.BlockSpec(memory_space=pltpu.SMEM)
    blk = jax.ShapeDtypeStruct((NS, ST, D), F32)
    anywhere = pl.BlockSpec(memory_space=pl.ANY)
    own_sizes = [(TOK - r0, n) for r0, n in GROUPS]
    far_sizes = [(r0 + n, n) for r0, n in GROUPS]
    V = pltpu.VMEM
    scratch = [
        V((4, NS, ST, D), F32), V((2, 2, TOK, D), F32), V((2, 3, 2, TOK, D), F32),
        V((2, 2, TOK, 2 * D), BF16), V((2, 2, TOK, 3 * D), BF16), V((2, 2, TOK, 2 * D), BF16),
        V((2, 2, 7, 256, 2 * D), BF16),
    ]
    scratch += [V(s, F32) for s in own_sizes] + [V(s, F32) for s in far_sizes]
    scratch += [V(s, F32) for s in own_sizes + far_sizes + far_sizes]
    scratch += [V((7, TOK, 256), F32)] * 4
    scratch += [V((TOK, D), F32)] * 2 + [V((TOK, 2 * D), F32)] * 3
    scratch += [V((8, 128), F32)] * 2
    scratch += [V((2, 8, TOK), F32), V((3, 2, 8, TOK), F32)]
    scratch += [V((512, 7 * 256), BF16)] * 2
    scratch += [
        pltpu.SemaphoreType.DMA((6, 4)), pltpu.SemaphoreType.DMA((2, 3, 4)),
        pltpu.SemaphoreType.DMA((3, 4)), pltpu.SemaphoreType.DMA((3, 4)),
        pltpu.SemaphoreType.DMA((4,)), pltpu.SemaphoreType.DMA((4,)),
    ]
    params = dict(vmem_limit_bytes=63 * 2**20)
    if comm:
        params.update(collective_id=0, has_side_effects=True)
    results = pl.pallas_call(
        functools.partial(kernel, total_devices, comm),
        out_shape=[blk] * 4,
        in_specs=[smem] + [anywhere] * 4,
        out_specs=[anywhere] * 4,
        scratch_shapes=scratch,
        compiler_params=pltpu.CompilerParams(**params),
        name="windowed_attention",
    )(stretch_order, *(x.reshape(NS, ST, D) for x in (queries, keys, values, out_grad)))
    results = pl.pallas_call(
        unsort_kernel,
        out_shape=[blk] * 4,
        in_specs=[smem] + [vmem] * 4,
        out_specs=[vmem] * 4,
        name="by_array",
    )(stretch_order, *results)
    return tuple(x.reshape(1, TOK, D) for x in results)


def solution(mesh):
    spec = P("outer", "inner", None)
    total = mesh.shape["outer"] * mesh.shape["inner"]
    return jax.shard_map(
        functools.partial(attention, total, True), mesh=mesh,
        in_specs=(spec, spec, spec, spec, P("outer", "inner")),
        out_specs=(spec,) * 4, check_vma=False,
    )
```

time: 72.9 us -> 61.8 us (0.85)
  the two profiles are of different devices: /device:TPU:1 before, /device:TPU:4 now
where the time goes in v1:
time: 61.8 us; the launch traced here: 61.6 us
  Pallas kernels  61 us (99%)
  between operations  0.64 us (1%)
    pallas_call x1, Pallas kernels, attention(): pl.pallas_call(functools.partial(kernel, total_devices, comm), out_shape=...  58.2 us
    pallas_call x1, Pallas kernels, attention(): pl.pallas_call(unsort_kernel, out_shape=[blk] * 4, in_specs=[smem] + [vme...  2.79 us

profile of v1, /device:TPU:4, one launch (start us, length us, event | category | flops | bytes accessed | tf_op | source)
XLA Modules:
  0.0 61.6 jit_solution(1521228751501419913)
XLA Ops:
  0.6 58.2 %windowed_attention.1 = (f32[7,128,128]{2,1,0:T(8,128)}, f32[7,128,128]{2,1,0:T(8,128)}, f32[7,128,128]{2,1,0:T(8,128)}, f32[7,128,128]{2,1,0:T(8,128)}) custom-call(s32[1,7]{1,0:T(1,128)} %order_ref.3, f32[7,128,128]{2,1,0:T(8,128)} %bitcast.8, f32[7,128,128]{2,1,0:T(8,128)} %bitcast.9, f32[7,128,128]{2,1,0:T(8,128)} %bitcast.10, f32[7,128,128]{2,1,0:T(8,128)} %bitcast.11), custom_call_target="tpu_custom_call" | custom-call | tf_op jit(solution)/shard_map/windowed_attention/pallas_call | solution.py:494
  58.8 2.8 %by_array.1 = (f32[7,128,128]{2,1,0:T(8,128)}, f32[7,128,128]{2,1,0:T(8,128)}, f32[7,128,128]{2,1,0:T(8,128)}, f32[7,128,128]{2,1,0:T(8,128)}) custom-call(s32[1,7]{1,0:T(1,128)} %order_ref.3, f32[7,128,128]{2,1,0:T(8,128)} %get-tuple-element.12.refs_0_, f32[7,128,128]{2,1,0:T(8,128)} %get-tuple-element.13.refs_1_, ...), custom_call_target="tpu_custom_call" | custom-call | tf_op jit(solution)/shard_map/by_array/pallas_call | solution.py:503
